TPU v7x, 256 devices: a whole 4x4x8 slice. The times are simulated.
256 devices in a mesh: tok: 32 (over x_lo, z, core), feat: 8 (over x_hi, y).
Axes of the slice: x: 4 (x_hi: 2, x_lo: 2; x = x_hi * 2 + x_lo), y: 4, z: 8, core: 2. Of those that a mesh axis runs over, the one named last changes fastest.
Arguments:
- teacher: bfloat16 [8192, 8192], P('tok', 'feat')
- student: bfloat16 [8192, 5120], P('tok', 'feat')
Outputs:
- loss: float32 [], replicated
- grad_student: float32 [8192, 5120], P('tok', 'feat')
All inputs are finite; a program needn't handle non-finite values.
Results may differ from a plain program's by a relative error of at most 0.0031.
Values may be sent and summed in bfloat16 or wider, within the bound.
A program may use at most 128 MiB of HBM per device.

v0:
```python
import jax
import jax.numpy as jnp
from jax import lax
from jax.sharding import PartitionSpec as P

DS = 5120


def gram_tile(rows, mine):
    return lax.dot_general(rows, mine, (((1,), (1,)), ((), ())), preferred_element_type=jnp.float32)


def local(teacher, student):
    width = teacher.shape[0]
    all_teacher, all_student = (
        lax.all_gather(teacher, "tok", axis=0, tiled=True),
        lax.all_gather(student, "tok", axis=0, tiled=True),
    )
    parts = lax.psum_scatter(
        jnp.concatenate([gram_tile(all_teacher, teacher), gram_tile(all_student, student)], axis=1),
        "feat",
        scatter_dimension=0,
        tiled=True,
    )
    kern = parts[:, :width]
    lern = parts[:, width:]
    local_sums = (jnp.sum(kern * lern), jnp.sum(kern * kern), jnp.sum(lern * lern))
    cross, ksq, lsq = lax.psum((local_sums[0], local_sums[1], local_sums[2]), ("tok", "feat"))
    knorm = jnp.sqrt(ksq)
    lnorm = jnp.sqrt(lsq)
    loss = -cross / (knorm * lnorm)
    weights = (-kern / (knorm * lnorm) + cross * lern / (knorm * lnorm**3)).astype(jnp.bfloat16)
    full_weights = lax.all_gather(weights, "feat", axis=0, tiled=True)
    scale = 2.0 * all_student.shape[0] * DS
    grad_student = scale * lax.dot_general(
        full_weights, all_student, (((0,), (0,)), ((), ())), preferred_element_type=jnp.float32
    )
    return (loss, grad_student)


def solution(mesh):
    placed = (P("tok", "feat"), P("tok", "feat"))
    return jax.shard_map(
        local, mesh=mesh, in_specs=placed, out_specs=(P(), P("tok", "feat")), check_vma=False
    )
```

profile of v0, /device:TPU:1, one launch (start us, length us, event | category | flops | bytes accessed | tf_op | source)
XLA Modules:
  0.0 575.2 jit_solution(16910604198474393018)
XLA Ops:
  7.2 0.0 all-gather.6.cloned.1.call-start
  7.2 0.7 all-gather.6.cloned.1.call-update
  7.9 0.0 all-gather.4.cloned.1.call-start
  7.9 0.7 all-gather.4.cloned.1.call-update
  8.6 0.0 copy-start.1
  8.7 0.0 reduce-scatter.2.cloned.1.call-start
  8.7 80.1 %all-gather.6.cloned.1.call-done = bf16[8192,640]{1,0:T(8,128)(2,1)} async-done(((bf16[256,640]{1,0:T(8,128)(2,1)}), bf16[8192,640]{1,0:T(8,128)(2,1)}) %all-gather.6.cloned.1.call-update) | async-done | bytes 10485776 | tf_op jit(solution)/shard_map/all_gather | solution.py:17
  88.8 10.7 %fusion.1 = f32[8192,256]{0,1:T(8,128)} fusion(bf16[8192,640]{1,0:T(8,128)(2,1)} %all-gather.6.cloned.1.call-done, bf16[256,640]{1,0:T(8,128)(2,1)} %param.3), kind=kOutput, calls=%fused_computation.7 | convolution fusion | flops 2684354560 | bytes 19202048 | tf_op jit(solution)/shard_map/dot_general | solution.py:10
  99.5 90.2 %all-gather.4.cloned.1.call-done = bf16[8192,1024]{1,0:T(8,128)(2,1)} async-done(((bf16[256,1024]{1,0:T(8,128)(2,1)}), bf16[8192,1024]{1,0:T(8,128)(2,1)}) %all-gather.4.cloned.1.call-update) | async-done | bytes 16777232 | tf_op jit(solution)/shard_map/all_gather | solution.py:16
  189.8 0.0 copy-done.1
  189.8 0.0 copy-start
  189.8 8.3 %fusion = f32[8192,256]{0,1:T(8,128)S(1)} fusion(bf16[8192,1024]{1,0:T(8,128)(2,1)} %all-gather.4.cloned.1.call-done, bf16[256,1024]{1,0:T(8,128)(2,1)S(1)} %copy-done.1), kind=kOutput, calls=%fused_computation.6 | convolution fusion | flops 4294967296 | bytes 25690112 | tf_op jit(solution)/shard_map/dot_general | solution.py:10
  198.1 0.0 copy-done
  198.1 6.2 %pad_maximum_fusion = f32[8192,512]{0,1:T(8,128)} fusion(f32[8192,256]{0,1:T(8,128)S(1)} %copy-done, f32[8192,256]{0,1:T(8,128)S(1)} %fusion), kind=kLoop, calls=%fused_computation | loop fusion | flops 4194304 | bytes 33554432 | tf_op jit(solution)/shard_map/concatenate | solution.py:20
  204.3 0.0 reduce-scatter.2.cloned.1.call-update
  204.3 0.0 all-gather.8.cloned.1.call-start
  204.4 195.3 %reduce-scatter.2.cloned.1.call-done = f32[1024,512]{0,1:T(8,128)} async-done(((f32[8192,512]{0,1:T(8,128)}), f32[1024,512]{0,1:T(8,128)}) %reduce-scatter.2.cloned.1.call-update) | async-done | bytes 2097168 | tf_op jit(solution)/shard_map/reduce_scatter | solution.py:19
  399.7 2.4 multiply_reduce_fusion
  402.1 78.7 %all-reduce = (f32[]{:T(128)}, f32[]{:T(128)}, f32[]{:T(128)}) all-reduce(f32[]{:T(128)} %get-tuple-element.3, f32[]{:T(128)} %get-tuple-element.4, f32[]{:T(128)} %get-tuple-element.2), channel_id=1, replica_groups=mesh['tok'=32,'feat'=8] {'tok','feat'}, use_global_device_ids=true, to_apply=%region_2.0 | all-reduce | flops 3 | bytes 24 | tf_op jit(solution)/shard_map/psum | solution.py:28
  482.2 3.3 add_convert_fusion
  485.5 0.0 all-gather.8.cloned.1.call-update
  486.3 71.7 %all-gather.8.cloned.1.call-done = bf16[8192,256]{0,1:T(8,128)(2,1)} async-done(((bf16[1024,256]{0,1:T(8,128)(2,1)}), bf16[8192,256]{0,1:T(8,128)(2,1)}) %all-gather.8.cloned.1.call-update) | async-done | bytes 4194320 | tf_op jit(solution)/shard_map/all_gather | solution.py:33
  558.0 9.5 %convolution_multiply_fusion = f32[256,640]{1,0:T(8,128)} fusion(bf16[8192,256]{0,1:T(8,128)(2,1)} %all-gather.8.cloned.1.call-done, bf16[8192,640]{1,0:T(8,128)(2,1)} %all-gather.6.cloned.1.call-done), kind=kOutput, calls=%fused_computation.1 | convolution fusion | flops 2684518400 | bytes 15335424 | tf_op jit(solution)/shard_map/dot_general | solution.py:35
Async XLA Ops:
  7.2 81.7 %all-gather.6.cloned.1.call-start = ((), (), s32[]{:S(2)}) async-start(), calls=%async_computation.2 | async-start | bytes 10813440 | tf_op jit(solution)/shard_map/all_gather | solution.py:17
  7.9 181.9 %all-gather.4.cloned.1.call-start = ((), (), s32[]{:S(2)}) async-start(), calls=%async_computation.1 | async-start | bytes 17301504 | tf_op jit(solution)/shard_map/all_gather | solution.py:16
  8.6 181.1 %copy-start.1 = (bf16[256,1024]{1,0:T(8,128)(2,1)S(1)}, bf16[256,1024]{1,0:T(8,128)(2,1)}, u32[]{:S(2)}) copy-start(bf16[256,1024]{1,0:T(8,128)(2,1)} %param.2) | copy-start | bytes 1572868
  8.7 391.0 %reduce-scatter.2.cloned.1.call-start = ((), (), s32[]{:S(2)}) async-start(), calls=%async_computation.3 | async-start | bytes 18874368 | tf_op jit(solution)/shard_map/reduce_scatter | solution.py:19
  189.8 8.3 %copy-start = (f32[8192,256]{0,1:T(8,128)S(1)}, f32[8192,256]{0,1:T(8,128)}, u32[]{:S(2)}) copy-start(f32[8192,256]{0,1:T(8,128)} %fusion.1) | copy-start | bytes 25165828
  204.3 353.6 %all-gather.8.cloned.1.call-start = ((), (), s32[]{:S(2)}) async-start(), calls=%async_computation.4 | async-start | bytes 4718592 | tf_op jit(solution)/shard_map/all_gather | solution.py:33
Sparse Core Ops, SparseCore 0:
  9.9 78.9 all-gather.5
  90.7 99.0 all-gather.3
  204.5 195.1 reduce-scatter.1
  485.6 72.2 all-gather.7
where the time goes:
time: 575 us
  waiting for transfers between devices  439 us (76%)
  blocking collectives  78.7 us (14%)
  matrix products  28.5 us (5%)
  between operations  17 us (3%)
  other arithmetic  11.9 us (2%)
    reduce_scatter x1, waiting for transfers between devices, local(): lax.psum_scatter(jnp.concatenate([gram_tile(all_teacher, teacher), gram_t...  195 us
    all_gather x1, waiting for transfers between devices, local(): lax.all_gather(teacher, 'tok', axis=0, tiled=True)  90.2 us
    all_gather x1, waiting for transfers between devices, local(): lax.all_gather(student, 'tok', axis=0, tiled=True)  80.1 us
    psum x1, blocking collectives, local(): lax.psum((local_sums[0], local_sums[1], local_sums[2]), ('tok', 'feat'))  78.7 us
    all_gather x1, waiting for transfers between devices, local(): full_weights = lax.all_gather(weights, 'feat', axis=0, tiled=True)  71.7 us
    dot_general x2, matrix products, gram_tile(): lax.dot_general(rows, mine, (((1,), (1,)), ((), ())), preferred_element_t...  19 us
  transfers between devices with their start and end apart: 4, of which 4 were waited for; matrix products, arithmetic and copies ran while one was open for 2% of the time, Pallas kernels for 0%

commit v1 on v0

--- a/solution.py
+++ b/solution.py
@@ -2,6 +2,7 @@
 import jax.numpy as jnp
 from jax import lax
 from jax.sharding import PartitionSpec as P
+from jax.lax import all_to_all, axis_size
 
 DS = 5120
 
@@ -30,7 +31,13 @@
     lnorm = jnp.sqrt(lsq)
     loss = -cross / (knorm * lnorm)
     weights = (-kern / (knorm * lnorm) + cross * lern / (knorm * lnorm**3)).astype(jnp.bfloat16)
-    full_weights = lax.all_gather(weights, "feat", axis=0, tiled=True)
+    field_out = all_to_all(
+        jnp.stack([weights for _ in range(axis_size("feat"))], 0),
+        "feat",
+        split_axis=0,
+        concat_axis=0,
+    )
+    full_weights = jnp.concatenate(field_out, 0)
     scale = 2.0 * all_student.shape[0] * DS
     grad_student = scale * lax.dot_general(
         full_weights, all_student, (((0,), (0,)), ((), ())), preferred_element_type=jnp.float32

time: 575 us -> 558 us (0.970)
  waiting for transfers between devices: 439 us -> 415 us
    all_gather x1 -> x0, waiting for transfers between devices: 71.7 us -> none  [local(): full_weights = lax.all_gather(weights, 'feat', axis=0, tiled=True)]
    all_to_all x0 -> x1, waiting for transfers between devices: none -> 47.9 us  [local(): all_to_all(jnp.stack([weights for _ in range(axis_size('feat'))], 0), 'fe...]
where the time goes in v1:
time: 558 us
  waiting for transfers between devices  415 us (74%)
  blocking collectives  78.7 us (14%)
  matrix products  28.5 us (5%)
  between operations  17 us (3%)
  other arithmetic  11.1 us (2%)
    reduce_scatter x1, waiting for transfers between devices, local(): lax.psum_scatter(jnp.concatenate([gram_tile(all_teacher, teacher), gram_t...  195 us
    all_gather x1, waiting for transfers between devices, local(): lax.all_gather(teacher, 'tok', axis=0, tiled=True)  90.2 us
    all_gather x1, waiting for transfers between devices, local(): lax.all_gather(student, 'tok', axis=0, tiled=True)  80.1 us
    psum x1, blocking collectives, local(): lax.psum((local_sums[0], local_sums[1], local_sums[2]), ('tok', 'feat'))  78.7 us
    all_to_all x1, waiting for transfers between devices, local(): all_to_all(jnp.stack([weights for _ in range(axis_size('feat'))], 0), 'fe...  47.9 us
    dot_general x2, matrix products, gram_tile(): lax.dot_general(rows, mine, (((1,), (1,)), ((), ())), preferred_element_t...  19 us
  transfers between devices with their start and end apart: 4, of which 4 were waited for; matrix products, arithmetic and copies ran while one was open for 2% of the time, Pallas kernels for 0%

profile of v1, /device:TPU:1, one launch (start us, length us, event | category | flops | bytes accessed | tf_op | source)
XLA Modules:
  0.0 557.5 jit_solution(4334936151077504822)
XLA Ops:
  7.2 0.0 all-gather.5.cloned.1.call-start
  7.2 0.7 all-gather.5.cloned.1.call-update
  7.9 0.0 all-gather.3.cloned.1.call-start
  7.9 0.7 all-gather.3.cloned.1.call-update
  8.6 0.0 copy-start.1
  8.7 0.0 reduce-scatter.2.cloned.1.call-start
  8.7 80.1 %all-gather.5.cloned.1.call-done = bf16[8192,640]{1,0:T(8,128)(2,1)} async-done(((bf16[256,640]{1,0:T(8,128)(2,1)}), bf16[8192,640]{1,0:T(8,128)(2,1)}) %all-gather.5.cloned.1.call-update) | async-done | bytes 10485776 | tf_op jit(solution)/shard_map/all_gather | solution.py:18
  88.8 10.7 %fusion.1 = f32[8192,256]{0,1:T(8,128)} fusion(bf16[8192,640]{1,0:T(8,128)(2,1)} %all-gather.5.cloned.1.call-done, bf16[256,640]{1,0:T(8,128)(2,1)} %param.3), kind=kOutput, calls=%fused_computation.7 | convolution fusion | flops 2684354560 | bytes 19202048 | tf_op jit(solution)/shard_map/dot_general | solution.py:11
  99.5 90.2 %all-gather.3.cloned.1.call-done = bf16[8192,1024]{1,0:T(8,128)(2,1)} async-done(((bf16[256,1024]{1,0:T(8,128)(2,1)}), bf16[8192,1024]{1,0:T(8,128)(2,1)}) %all-gather.3.cloned.1.call-update) | async-done | bytes 16777232 | tf_op jit(solution)/shard_map/all_gather | solution.py:17
  189.8 0.0 copy-done.1
  189.8 0.0 copy-start
  189.8 8.3 %fusion = f32[8192,256]{0,1:T(8,128)S(1)} fusion(bf16[8192,1024]{1,0:T(8,128)(2,1)} %all-gather.3.cloned.1.call-done, bf16[256,1024]{1,0:T(8,128)(2,1)S(1)} %copy-done.1), kind=kOutput, calls=%fused_computation.6 | convolution fusion | flops 4294967296 | bytes 25690112 | tf_op jit(solution)/shard_map/dot_general | solution.py:11
  198.1 0.0 copy-done
  198.1 6.3 %pad_maximum_fusion = f32[8192,512]{0,1:T(8,128)} fusion(f32[8192,256]{0,1:T(8,128)S(1)} %copy-done, f32[8192,256]{0,1:T(8,128)S(1)} %fusion), kind=kLoop, calls=%fused_computation | loop fusion | flops 4194304 | bytes 33554432 | tf_op jit(solution)/shard_map/concatenate | solution.py:21
  204.4 0.0 reduce-scatter.2.cloned.1.call-update
  204.4 195.4 %reduce-scatter.2.cloned.1.call-done = f32[1024,512]{0,1:T(8,128)} async-done(((f32[8192,512]{0,1:T(8,128)}), f32[1024,512]{0,1:T(8,128)}) %reduce-scatter.2.cloned.1.call-update) | async-done | bytes 2097168 | tf_op jit(solution)/shard_map/reduce_scatter | solution.py:20
  399.8 2.4 multiply_reduce_fusion
  402.2 78.7 %all-reduce = (f32[]{:T(128)}, f32[]{:T(128)}, f32[]{:T(128)}) all-reduce(f32[]{:T(128)} %get-tuple-element.3, f32[]{:T(128)} %get-tuple-element.4, f32[]{:T(128)} %get-tuple-element.2), channel_id=1, replica_groups=mesh['tok'=32,'feat'=8] {'tok','feat'}, use_global_device_ids=true, to_apply=%region_2.0 | all-reduce | flops 3 | bytes 24 | tf_op jit(solution)/shard_map/psum | solution.py:29
  482.3 2.4 add_convert_fusion
  484.7 0.2 copy.4
  484.9 2.2 stack.2
  487.2 4.5 all-to-all-start
  492.4 47.9 %all-to-all-done = bf16[8,1024,256]{2,1,0:T(8,128)(2,1)} async-done(((bf16[8,1024,256]{2,1,0:T(8,128)(2,1)}), bf16[8,1024,256]{2,1,0:T(8,128)(2,1)}, u32[]{:S(2)}, u32[]{:S(2)}) %all-to-all-start) | async-done | bytes 4194336 | tf_op jit(solution)/shard_map/all_to_all | solution.py:34
  540.3 9.6 %convolution_multiply_fusion = f32[256,640]{1,0:T(8,128)} fusion(bf16[8192,256]{1,0:T(8,128)(2,1)} %bitcast, bf16[8192,640]{1,0:T(8,128)(2,1)} %all-gather.5.cloned.1.call-done), kind=kOutput, calls=%fused_computation.1 | convolution fusion | flops 2684518400 | bytes 15335424 | tf_op jit(solution)/shard_map/dot_general | solution.py:42
Async XLA Ops:
  7.2 81.7 %all-gather.5.cloned.1.call-start = ((), (), s32[]{:S(2)}) async-start(), calls=%async_computation.3 | async-start | bytes 10813440 | tf_op jit(solution)/shard_map/all_gather | solution.py:18
  7.9 181.9 %all-gather.3.cloned.1.call-start = ((), (), s32[]{:S(2)}) async-start(), calls=%async_computation.2 | async-start | bytes 17301504 | tf_op jit(solution)/shard_map/all_gather | solution.py:17
  8.6 181.1 %copy-start.1 = (bf16[256,1024]{1,0:T(8,128)(2,1)S(1)}, bf16[256,1024]{1,0:T(8,128)(2,1)}, u32[]{:S(2)}) copy-start(bf16[256,1024]{1,0:T(8,128)(2,1)} %param.2) | copy-start | bytes 1572868
  8.7 391.1 %reduce-scatter.2.cloned.1.call-start = ((), (), s32[]{:S(2)}) async-start(), calls=%async_computation.4 | async-start | bytes 18874368 | tf_op jit(solution)/shard_map/reduce_scatter | solution.py:20
  189.8 8.3 %copy-start = (f32[8192,256]{0,1:T(8,128)S(1)}, f32[8192,256]{0,1:T(8,128)}, u32[]{:S(2)}) copy-start(f32[8192,256]{0,1:T(8,128)} %fusion.1) | copy-start | bytes 25165828
  487.2 53.2 %all-to-all-start = ((bf16[8,1024,256]{2,1,0:T(8,128)(2,1)}), bf16[8,1024,256]{2,1,0:T(8,128)(2,1)}, u32[]{:S(2)}, u32[]{:S(2)}) async-start(bf16[8,1024,256]{2,1,0:T(8,128)(2,1)} %stack.2), calls=%async_computation.1 | async-start | bytes 8388608 | tf_op jit(solution)/shard_map/all_to_all | solution.py:34
Sparse Core Ops, SparseCore 0:
  9.9 78.9 all-gather.4
  90.7 99.0 all-gather.2
  204.5 195.1 reduce-scatter.1

commit v2 on v0

--- a/solution.py
+++ b/solution.py
@@ -2,6 +2,7 @@
 import jax.numpy as jnp
 from jax import lax
 from jax.sharding import PartitionSpec as P
+from jax.lax import psum
 
 DS = 5120
 
@@ -25,7 +26,9 @@
     kern = parts[:, :width]
     lern = parts[:, width:]
     local_sums = (jnp.sum(kern * lern), jnp.sum(kern * kern), jnp.sum(lern * lern))
-    cross, ksq, lsq = lax.psum((local_sums[0], local_sums[1], local_sums[2]), ("tok", "feat"))
+    cross, ksq, lsq = psum(
+        psum((local_sums[0], local_sums[1], local_sums[2]), axis_name="tok"), axis_name="feat"
+    )
     knorm = jnp.sqrt(ksq)
     lnorm = jnp.sqrt(lsq)
     loss = -cross / (knorm * lnorm)

time: 575 us -> 571 us (level)
    psum x1 -> x2, blocking collectives: 78.7 us -> 76.2 us  [the longest x1 57 us: local(): psum((local_sums[0], local_sums[1], local_sums[2]), axis_name='tok')]
where the time goes in v2:
time: 571 us
  waiting for transfers between devices  438 us (77%)
  blocking collectives  76.2 us (13%)
  matrix products  28.5 us (5%)
  between operations  16.9 us (3%)
  other arithmetic  11.8 us (2%)
    reduce_scatter x1, waiting for transfers between devices, local(): lax.psum_scatter(jnp.concatenate([gram_tile(all_teacher, teacher), gram_t...  194 us
    all_gather x1, waiting for transfers between devices, local(): lax.all_gather(teacher, 'tok', axis=0, tiled=True)  90.2 us
    all_gather x1, waiting for transfers between devices, local(): lax.all_gather(student, 'tok', axis=0, tiled=True)  80.1 us
    all_gather x1, waiting for transfers between devices, local(): full_weights = lax.all_gather(weights, 'feat', axis=0, tiled=True)  71.8 us
    psum x1, blocking collectives, local(): psum((local_sums[0], local_sums[1], local_sums[2]), axis_name='tok')  57 us
    psum x1, blocking collectives, local(): psum(psum((local_sums[0], local_sums[1], local_sums[2]), axis_name='tok')...  19.2 us
    dot_general x2, matrix products, gram_tile(): lax.dot_general(rows, mine, (((1,), (1,)), ((), ())), preferred_element_t...  19 us
  transfers between devices with their start and end apart: 4, of which 4 were waited for; matrix products, arithmetic and copies ran while one was open for 2% of the time, Pallas kernels for 0%

profile of v2, /device:TPU:1, one launch (start us, length us, event | category | flops | bytes accessed | tf_op | source)
XLA Modules:
  0.0 571.0 jit_solution(2836844664184944750)
XLA Ops:
  7.2 0.0 all-gather.6.cloned.1.call-start
  7.2 0.7 all-gather.6.cloned.1.call-update
  7.9 0.0 all-gather.4.cloned.1.call-start
  7.9 0.7 all-gather.4.cloned.1.call-update
  8.6 0.0 copy-start.1
  8.7 0.0 reduce-scatter.2.cloned.1.call-start
  8.7 80.1 %all-gather.6.cloned.1.call-done = bf16[8192,640]{1,0:T(8,128)(2,1)} async-done(((bf16[256,640]{1,0:T(8,128)(2,1)}), bf16[8192,640]{1,0:T(8,128)(2,1)}) %all-gather.6.cloned.1.call-update) | async-done | bytes 10485776 | tf_op jit(solution)/shard_map/all_gather | solution.py:18
  88.8 10.7 %fusion.1 = f32[8192,256]{0,1:T(8,128)} fusion(bf16[8192,640]{1,0:T(8,128)(2,1)} %all-gather.6.cloned.1.call-done, bf16[256,640]{1,0:T(8,128)(2,1)} %param.3), kind=kOutput, calls=%fused_computation.7 | convolution fusion | flops 2684354560 | bytes 19202048 | tf_op jit(solution)/shard_map/dot_general | solution.py:11
  99.5 90.2 %all-gather.4.cloned.1.call-done = bf16[8192,1024]{1,0:T(8,128)(2,1)} async-done(((bf16[256,1024]{1,0:T(8,128)(2,1)}), bf16[8192,1024]{1,0:T(8,128)(2,1)}) %all-gather.4.cloned.1.call-update) | async-done | bytes 16777232 | tf_op jit(solution)/shard_map/all_gather | solution.py:17
  189.8 0.0 copy-done.1
  189.8 0.0 copy-start
  189.8 8.3 %fusion = f32[8192,256]{0,1:T(8,128)S(1)} fusion(bf16[8192,1024]{1,0:T(8,128)(2,1)} %all-gather.4.cloned.1.call-done, bf16[256,1024]{1,0:T(8,128)(2,1)S(1)} %copy-done.1), kind=kOutput, calls=%fused_computation.6 | convolution fusion | flops 4294967296 | bytes 25690112 | tf_op jit(solution)/shard_map/dot_general | solution.py:11
  198.1 0.0 copy-done
  198.1 6.2 %pad_maximum_fusion = f32[8192,512]{0,1:T(8,128)} fusion(f32[8192,256]{0,1:T(8,128)S(1)} %copy-done, f32[8192,256]{0,1:T(8,128)S(1)} %fusion), kind=kLoop, calls=%fused_computation | loop fusion | flops 4194304 | bytes 33554432 | tf_op jit(solution)/shard_map/concatenate | solution.py:21
  204.3 0.0 reduce-scatter.2.cloned.1.call-update
  204.3 0.0 all-gather.8.cloned.1.call-start
  204.4 193.9 %reduce-scatter.2.cloned.1.call-done = f32[1024,512]{0,1:T(8,128)} async-done(((f32[8192,512]{0,1:T(8,128)}), f32[1024,512]{0,1:T(8,128)}) %reduce-scatter.2.cloned.1.call-update) | async-done | bytes 2097168 | tf_op jit(solution)/shard_map/reduce_scatter | solution.py:20
  398.3 2.4 multiply_reduce_fusion
  400.7 57.0 %all-reduce = (f32[]{:T(128)}, f32[]{:T(128)}, f32[]{:T(128)}) all-reduce(f32[]{:T(128)} %get-tuple-element.3, f32[]{:T(128)} %get-tuple-element.4, f32[]{:T(128)} %get-tuple-element.2), channel_id=1, replica_groups=mesh['tok'=32,'feat'=8] {'tok'}, use_global_device_ids=true, to_apply=%region_2.0 | all-reduce | flops 3 | bytes 24 | tf_op jit(solution)/shard_map/psum | solution.py:30
  457.7 19.2 %all-reduce.1 = (f32[]{:T(128)}, f32[]{:T(128)}, f32[]{:T(128)}) all-reduce(f32[]{:T(128)} %get-tuple-element.5, f32[]{:T(128)} %get-tuple-element.6, f32[]{:T(128)} %get-tuple-element.7), channel_id=1, replica_groups=mesh['tok'=32,'feat'=8] {'feat'}, use_global_device_ids=true, to_apply=%region_3.0 | all-reduce | flops 3 | bytes 24 | tf_op jit(solution)/shard_map/psum | solution.py:29
  478.2 3.2 add_convert_fusion
  481.4 0.0 all-gather.8.cloned.1.call-update
  482.1 71.8 %all-gather.8.cloned.1.call-done = bf16[8192,256]{0,1:T(8,128)(2,1)} async-done(((bf16[1024,256]{0,1:T(8,128)(2,1)}), bf16[8192,256]{0,1:T(8,128)(2,1)}) %all-gather.8.cloned.1.call-update) | async-done | bytes 4194320 | tf_op jit(solution)/shard_map/all_gather | solution.py:36
  553.9 9.5 %convolution_multiply_fusion = f32[256,640]{1,0:T(8,128)} fusion(bf16[8192,256]{0,1:T(8,128)(2,1)} %all-gather.8.cloned.1.call-done, bf16[8192,640]{1,0:T(8,128)(2,1)} %all-gather.6.cloned.1.call-done), kind=kOutput, calls=%fused_computation.1 | convolution fusion | flops 2684518400 | bytes 15335424 | tf_op jit(solution)/shard_map/dot_general | solution.py:38
Async XLA Ops:
  7.2 81.7 %all-gather.6.cloned.1.call-start = ((), (), s32[]{:S(2)}) async-start(), calls=%async_computation.2 | async-start | bytes 10813440 | tf_op jit(solution)/shard_map/all_gather | solution.py:18
  7.9 181.9 %all-gather.4.cloned.1.call-start = ((), (), s32[]{:S(2)}) async-start(), calls=%async_computation.1 | async-start | bytes 17301504 | tf_op jit(solution)/shard_map/all_gather | solution.py:17
  8.6 181.1 %copy-start.1 = (bf16[256,1024]{1,0:T(8,128)(2,1)S(1)}, bf16[256,1024]{1,0:T(8,128)(2,1)}, u32[]{:S(2)}) copy-start(bf16[256,1024]{1,0:T(8,128)(2,1)} %param.2) | copy-start | bytes 1572868
  8.7 389.6 %reduce-scatter.2.cloned.1.call-start = ((), (), s32[]{:S(2)}) async-start(), calls=%async_computation.3 | async-start | bytes 18874368 | tf_op jit(solution)/shard_map/reduce_scatter | solution.py:20
  189.8 8.3 %copy-start = (f32[8192,256]{0,1:T(8,128)S(1)}, f32[8192,256]{0,1:T(8,128)}, u32[]{:S(2)}) copy-start(f32[8192,256]{0,1:T(8,128)} %fusion.1) | copy-start | bytes 25165828
  204.3 349.5 %all-gather.8.cloned.1.call-start = ((), (), s32[]{:S(2)}) async-start(), calls=%async_computation.4 | async-start | bytes 4718592 | tf_op jit(solution)/shard_map/all_gather | solution.py:36
Sparse Core Ops, SparseCore 0:
  9.9 78.9 all-gather.5
  90.7 99.0 all-gather.3
  204.4 193.8 reduce-scatter.1
  481.5 72.2 all-gather.7
